TPU v7x, 32 devices: a whole 2x2x4 slice. The times are simulated.
32 devices in a mesh: lon: 8 (over y, x, core), lat: 4 (over z).
Axes of the slice: x: 2, y: 2, z: 4, core: 2. Of those that a mesh axis runs over, the one named last changes fastest.
Arguments:
- u_wind: float32 [16, 2880, 512], P(None, 'lon', 'lat'), may hold values from -6 to 6
- v_wind: float32 [16, 2880, 512], P(None, 'lon', 'lat'), may hold values from -6 to 6
- height: float32 [16, 2880, 512], P(None, 'lon', 'lat'), may hold values from -6 to 6
Outputs:
- u_next: float32 [16, 2880, 512], P(None, 'lon', 'lat')
- v_next: float32 [16, 2880, 512], P(None, 'lon', 'lat')
- height_next: float32 [16, 2880, 512], P(None, 'lon', 'lat')
All inputs are finite; a program needn't handle non-finite values.
Results may differ from a plain program's by a relative error of at most 0.00013.
Values sent between devices are 32-bit elements; how exact they have to be, the bound alone decides.
A program may use at most 192 MiB of HBM per device.

v0:
```python
import math

import jax
import jax.numpy as jnp
import numpy as np
from jax import lax
from jax.sharding import PartitionSpec as P

grav_zonal = 0.3
grav_merid = 0.6
coriolis = 0.8
divergence_coef = 0.3
diffusion = 0.08


def with_halo(value, sides, width, wrap):
    for axis, dim in sides:
        size, length = (lax.axis_size(axis), value.shape[dim])
        up = [(i, (i + 1) % size) for i in range(size if wrap else size - 1)]
        down = [(j, i) for i, j in up]
        last = lax.slice_in_dim(value, length - width, length, axis=dim)
        initial = lax.slice_in_dim(value, 0, width, axis=dim)
        before = lax.ppermute(last, axis, up)
        after = lax.ppermute(initial, axis, down)
        value = jnp.concatenate([before, value, after], axis=dim)
    return value


def from_behind(block, axis, distance):
    devices = range(lax.axis_size(axis))
    route = [((i - distance) % len(devices), i) for i in devices]
    return lax.ppermute(block, axis, route)


def shifted(field, row_step, col_step, row_count, col_count):
    return field[
        :, 1 + row_step : 1 + row_step + row_count, 1 + col_step : 1 + col_step + col_count
    ]


def stencil(padded, first_row, lat_total):
    row_count = padded.shape[2] - 2
    col_count = padded.shape[3] - 2
    height, u_wind, v_wind = (padded[0], padded[1], padded[2])

    def view(field, row_step, col_step):
        return shifted(field, row_step, col_step, row_count, col_count)

    def laplace(field):
        return (
            view(field, 0, 1)
            + view(field, 0, -1)
            + view(field, 1, 0)
            + view(field, -1, 0)
            - 4.0 * view(field, 0, 0)
        )

    lat_index = (first_row + jnp.arange(row_count)).astype(jnp.float32)[:, None]
    center = (lat_index + 0.5) * (math.pi / lat_total)
    cos_center = jnp.sin(center)
    sin_center = -jnp.cos(center)
    face = (lat_index + 1.0) * (math.pi / lat_total)
    sin_face = -jnp.cos(face)
    cos_face = jnp.where(lat_index + 1.0 < lat_total, jnp.sin(face), 0.0)
    cos_south = jnp.sin(lat_index * (math.pi / lat_total))
    u_next = (
        view(u_wind, 0, 0)
        - grav_zonal * (view(height, 0, 1) - view(height, 0, 0)) / cos_center
        + coriolis
        * sin_center
        * 0.25
        * (view(v_wind, 0, 0) + view(v_wind, 0, 1) + view(v_wind, -1, 0) + view(v_wind, -1, 1))
        + diffusion * laplace(u_wind)
    )
    v_next = (
        view(v_wind, 0, 0)
        - grav_merid * (view(height, 1, 0) - view(height, 0, 0))
        - coriolis
        * sin_face
        * 0.25
        * (view(u_wind, 0, 0) + view(u_wind, 0, -1) + view(u_wind, 1, 0) + view(u_wind, 1, -1))
        + diffusion * laplace(v_wind)
    )
    flux = (
        view(u_wind, 0, 0)
        - view(u_wind, 0, -1)
        + cos_face * view(v_wind, 0, 0)
        - cos_south * view(v_wind, -1, 0)
    )
    height_next = (
        view(height, 0, 0) - divergence_coef * flux / cos_center + diffusion * laplace(height)
    )
    return jnp.stack([height_next, u_next, v_next])


def fourier_tables(lon_total):
    freq_index = np.arange(lon_total)
    is_cosine = freq_index <= lon_total // 2
    wavenum = np.where(is_cosine, freq_index, freq_index - lon_total // 2)
    phase_index = wavenum[:, None] * np.arange(lon_total)[None, :] % lon_total
    angles = phase_index * (2.0 * math.pi / lon_total)
    basis_rows = np.where(is_cosine[:, None], np.cos(angles), np.sin(angles)).astype(np.float32)
    sine_vals = np.sin(wavenum * (math.pi / lon_total))
    sine_sq = (sine_vals * sine_vals).astype(np.float32)
    weight = (
        np.where((freq_index == 0) | (freq_index == lon_total // 2), 1.0, 2.0) / lon_total
    ).astype(np.float32)
    return (basis_rows, sine_sq, weight)


def polar_filter(circles, damp_ratio):
    lon_total = circles.shape[1]
    block_width = lon_total // 8
    basis_table, sine_table, weight_table = fourier_tables(lon_total)
    running = jnp.zeros_like(circles)
    for block_index in range(8):
        first = block_index * block_width
        basis_rows = jnp.asarray(basis_table[first : first + block_width])
        sine_sq = jnp.asarray(sine_table[first : first + block_width])
        weight = jnp.asarray(weight_table[first : first + block_width])
        spectra = jnp.dot(circles, basis_rows.T, precision=lax.Precision.HIGHEST)
        damping = damp_ratio / jnp.maximum(sine_sq[None, :], damp_ratio)
        running = running + jnp.dot(
            spectra * damping * weight[None, :], basis_rows, precision=lax.Precision.HIGHEST
        )
    return running


def shards(u_wind, v_wind, height):
    u_wind = jnp.swapaxes(u_wind, 1, 2)
    v_wind = jnp.swapaxes(v_wind, 1, 2)
    height = jnp.swapaxes(height, 1, 2)
    levels, row_count, col_count = height.shape
    n_lat = lax.axis_size("lat")
    n_lon = lax.axis_size("lon")
    lat_total = row_count * n_lat
    lat_band = lax.axis_index("lat")
    stacked = jnp.stack([height, u_wind, v_wind])
    lon_padded = with_halo(stacked, (("lon", 3),), 1, True)
    both_padded = with_halo(lon_padded, (("lat", 2),), 1, False)
    pole_rows = jnp.concatenate(
        [lon_padded[:, :, 0:1], lon_padded[:, :, row_count - 2 : row_count]], 2
    )
    across_pole = from_behind(pole_rows, "lon", n_lon // 2)
    flip_sign = jnp.array([1.0, -1.0], jnp.float32).reshape(2, 1, 1, 1)
    north_rows = jnp.concatenate(
        [across_pole[0:2, :, 2:3] * flip_sign, -across_pole[2:3, :, 1:2]], 0
    )
    south_rows = jnp.concatenate(
        [across_pole[0:2, :, 0:1] * flip_sign, jnp.zeros_like(across_pole[2:3, :, 0:1])], 0
    )
    lower_rim = jnp.where(lat_band == 0, south_rows, both_padded[:, :, 0:1])
    upper_rim = jnp.where(lat_band == n_lat - 1, north_rows, both_padded[:, :, row_count + 1 :])
    padded = jnp.concatenate([lower_rim, both_padded[:, :, 1 : row_count + 1], upper_rim], 2)
    stepped = stencil(padded, lat_band * row_count, lat_total)
    buffer = stepped.reshape(3, levels * row_count, col_count)
    is_polar = (lat_band < n_lat // 4) | (lat_band >= n_lat - n_lat // 4)
    arrived = lax.all_to_all(buffer, "lon", split_axis=1, concat_axis=2, tiled=True)
    item_count, row_span, lon_span = arrived.shape
    flat_index = 0 + lax.axis_index("lon") * row_span + jnp.arange(row_span, dtype=jnp.int32)
    lat_row = lat_band * row_count + flat_index % row_count
    cosine = jnp.sin((lat_row.astype(jnp.float32) + 0.5) * (math.pi / lat_total))
    damp_ratio = (2.0 * cosine * cosine)[:, None]
    smoothed = polar_filter(
        arrived.reshape(item_count * row_span, lon_span), jnp.tile(damp_ratio, (item_count, 1))
    )
    smoothed = lax.all_to_all(
        smoothed.reshape(item_count, row_span, lon_span),
        "lon",
        split_axis=2,
        concat_axis=1,
        tiled=True,
    )
    result = jnp.where(is_polar, smoothed, buffer)
    result = result.reshape(3, levels, row_count, col_count)
    return (
        jnp.swapaxes(result[1], 1, 2),
        jnp.swapaxes(result[2], 1, 2),
        jnp.swapaxes(result[0], 1, 2),
    )


def solution(mesh):
    placed = (P(None, "lon", "lat"), P(None, "lon", "lat"), P(None, "lon", "lat"))
    return jax.shard_map(
        shards,
        mesh=mesh,
        in_specs=placed,
        out_specs=(P(None, "lon", "lat"), P(None, "lon", "lat"), P(None, "lon", "lat")),
        check_vma=False,
    )
```

profile of v0, /device:TPU:0, one launch (start us, length us, event | category | flops | bytes accessed | tf_op | source)
XLA Modules:
  0.0 937.1 jit_solution(9673197077463121341)
XLA Ops:
  86.7 21.3 %pad_maximum_fusion = f32[3,16,130,362]{2,1,3,0:T(8,128)} fusion(f32[3,16,1,362]{2,1,3,0:T(8,128)} %broadcast_select_fusion, f32[3,16,128,1]{2,1,3,0:T(8,128)S(1)} %collective-permute-done.1, f32[1,16,128,360]{2,1,3,0:T(8,128)} %copy-done.2, f32[1,16,128,360]{2,1,3,0:T(8,128)} %copy-done.3, f32[1,16,128,360]{2,1,3,0:T(8,128)S(1)} %bitcast.95, ...), kind=kLoop, calls=%fused_computation | loop fusion | flops 13553280 | bytes 18071040 | tf_op jit(solution)/shard_map/concatenate | solution.py:154
  121.3 15.6 %fusion.14 = f32[16,128,360]{1,0,2:T(8,128)} fusion(f32[16,130,362]{1,0,2:T(8,128)} %get-tuple-element.20, f32[16,130,362]{1,0,2:T(8,128)} %get-tuple-element.19, f32[16,130,362]{1,0,2:T(8,128)S(1)} %get-tuple-element.18, f32[128]{0:T(128)S(1)} %fusion.31, f32[128]{0:T(128)S(1)} %get-tuple-element.35, f32[128]{0:T(128)S(1)} %get-tuple-element.32), kind=kLoop, calls=%fused_computation.33 | loop fusion | flops 11059200 | bytes 29492736 | tf_op jit(solution)/shard_map/add | solution.py:91
  139.7 22.6 %fusion.8 = f32[16,128,360]{1,0,2:T(8,128)} fusion(f32[16,130,362]{1,0,2:T(8,128)} %copy-done.1, f32[16,130,362]{1,0,2:T(8,128)} %get-tuple-element.19, f32[16,130,362]{1,0,2:T(8,128)} %get-tuple-element.20, f32[128]{0:T(128)S(1)} %get-tuple-element.34, f32[128]{0:T(128)S(1)} %fusion.31), kind=kLoop, calls=%fused_computation.24 | loop fusion | flops 11796480 | bytes 35390464 | tf_op jit(solution)/shard_map/add | solution.py:67
  162.3 27.9 %fusion.3 = f32[16,128,360]{1,0,2:T(8,128)} fusion(f32[16,130,362]{1,0,2:T(8,128)} %get-tuple-element.19, f32[16,130,362]{1,0,2:T(8,128)} %copy-done.1, f32[16,130,362]{1,0,2:T(8,128)} %get-tuple-element.20, f32[128]{0:T(128)S(1)} %get-tuple-element.33), kind=kLoop, calls=%fused_computation.16 | loop fusion | flops 11059200 | bytes 35389952 | tf_op jit(solution)/shard_map/add | solution.py:76
  206.3 12.8 %copy.96 = f32[3,2048,360]{2,0,1:T(4,128)} copy(f32[3,2048,360]{1,2,0:T(8,128)} %constant_dynamic-update-slice_fusion) | data formatting | bytes 17694720 | tf_op jit(solution)/shard_map/stack | solution.py:93
  224.7 138.9 %all-to-all-done = f32[3,2048,360]{2,0,1:T(4,128)} async-done(((f32[3,2048,360]{2,0,1:T(4,128)}), f32[3,2048,360]{2,0,1:T(4,128)}, u32[]{:S(2)}, u32[]{:S(2)}) %all-to-all-start) | async-done | bytes 8847392 | tf_op jit(solution)/shard_map/all_to_all | solution.py:158
  363.7 13.6 %copy.113 = f32[3,8,256,360]{3,1,2,0:T(8,128)} copy(f32[3,8,256,360]{3,0,2,1:T(4,128)} %bitcast.9) | data formatting | bytes 17694720 | tf_op jit(solution)/shard_map/all_to_all | solution.py:158
  388.8 14.2 %fusion.16 = f32[768,360]{0,1:T(8,128)S(1)} fusion(f32[768,2880]{1,0:T(8,128)} %reshape.124, f32[360,2880]{1,0:T(8,128)} %constant.106.clone, f32[360]{0:T(512)S(1)} %copy-done.12, f32[768]{0:T(1024)S(1)} %tile.9), kind=kOutput, calls=%fused_computation.40 | convolution fusion | flops 9556254720 | bytes 14104992 | tf_op jit(solution)/shard_map/dot_general | solution.py:121
  403.0 27.0 %fusion.20 = f32[768,360]{0,1:T(8,128)} fusion(f32[768,2880]{1,0:T(8,128)S(1)} %copy-done, f32[360,2880]{1,0:T(8,128)} %constant.100.clone, f32[360]{0:T(512)S(1)} %copy-done.12, f32[768]{0:T(1024)S(1)} %tile.9), kind=kOutput, calls=%fused_computation.48 | convolution fusion | flops 9556254720 | bytes 14104992 | tf_op jit(solution)/shard_map/dot_general | solution.py:121
  430.1 19.6 %fusion.17 = f32[768,360]{0,1:T(8,128)S(1)} fusion(f32[768,2880]{1,0:T(8,128)S(1)} %copy-done, f32[360,2880]{1,0:T(8,128)S(1)} %bitcast.105, f32[360]{0:T(512)S(1)} %copy-done.13, f32[768]{0:T(1024)S(1)} %tile.9), kind=kOutput, calls=%fused_computation.42 | convolution fusion | flops 9556254720 | bytes 14104992 | tf_op jit(solution)/shard_map/dot_general | solution.py:121
  449.8 20.3 %fusion.21 = f32[768,360]{0,1:T(8,128)} fusion(f32[768,2880]{1,0:T(8,128)S(1)} %copy-done, f32[360,2880]{1,0:T(8,128)S(1)} %bitcast.111, f32[360]{0:T(512)S(1)} %copy-done.13, f32[768]{0:T(1024)S(1)} %tile.9), kind=kOutput, calls=%fused_computation.50 | convolution fusion | flops 9556254720 | bytes 14104992 | tf_op jit(solution)/shard_map/dot_general | solution.py:121
  470.2 19.6 %fusion.18 = f32[768,360]{0,1:T(8,128)S(1)} fusion(f32[768,2880]{1,0:T(8,128)S(1)} %copy-done, f32[360,2880]{1,0:T(8,128)S(1)} %bitcast.107, f32[360]{0:T(512)S(1)} %copy-done.14, f32[768]{0:T(1024)S(1)} %tile.9), kind=kOutput, calls=%fused_computation.44 | convolution fusion | flops 9556254720 | bytes 14104992 | tf_op jit(solution)/shard_map/dot_general | solution.py:121
  489.9 20.1 %fusion.22 = f32[768,360]{0,1:T(8,128)} fusion(f32[768,2880]{1,0:T(8,128)S(1)} %copy-done, f32[360,2880]{1,0:T(8,128)S(1)} %bitcast.113, f32[360]{0:T(512)S(1)} %copy-done.14, f32[768]{0:T(1024)S(1)} %tile.9), kind=kOutput, calls=%fused_computation.52 | convolution fusion | flops 9556254720 | bytes 14104992 | tf_op jit(solution)/shard_map/dot_general | solution.py:121
  521.9 23.8 %fusion.33 = f32[768,2880]{0,1:T(8,128)} fusion(f32[768,360]{0,1:T(8,128)S(1)} %fusion.23, f32[360,2880]{1,0:T(8,128)S(1)} %bitcast.103), kind=kOutput, calls=%fused_computation.90 | convolution fusion | flops 9555148800 | bytes 14100480 | tf_op jit(solution)/shard_map/dot_general | solution.py:123
  545.7 25.6 %fusion.34 = f32[768,2880]{0,1:T(8,128)} fusion(f32[768,360]{0,1:T(8,128)S(1)} %copy-done.8, f32[360,2880]{1,0:T(8,128)S(1)} %bitcast.113), kind=kOutput, calls=%fused_computation.91 | convolution fusion | flops 9555148800 | bytes 14100480 | tf_op jit(solution)/shard_map/dot_general | solution.py:123
  571.3 23.7 %fusion.35 = f32[768,2880]{0,1:T(8,128)} fusion(f32[768,360]{0,1:T(8,128)S(1)} %copy-done.7, f32[360,2880]{1,0:T(8,128)S(1)} %bitcast.111), kind=kOutput, calls=%fused_computation.92 | convolution fusion | flops 9555148800 | bytes 14100480 | tf_op jit(solution)/shard_map/dot_general | solution.py:123
  595.1 25.4 %fusion.36 = f32[768,2880]{0,1:T(8,128)} fusion(f32[768,360]{0,1:T(8,128)S(1)} %copy-done.6, f32[360,2880]{1,0:T(8,128)S(1)} %bitcast.109), kind=kOutput, calls=%fused_computation.93 | convolution fusion | flops 9555148800 | bytes 14100480 | tf_op jit(solution)/shard_map/dot_general | solution.py:123
  620.5 11.8 %fusion.19 = f32[768,360]{0,1:T(8,128)S(1)} fusion(f32[768,2880]{1,0:T(8,128)S(1)} %copy-done, f32[360,2880]{1,0:T(8,128)S(1)} %bitcast.101, f32[360]{0:T(512)S(1)} %copy-done.15, f32[360]{0:T(512)S(1)} %copy-done.11, f32[768]{0:T(1024)S(1)} %tile.9), kind=kOutput, calls=%fused_computation.46 | convolution fusion | flops 9556254720 | bytes 14106432 | tf_op jit(solution)/shard_map/dot_general | solution.py:121
  632.4 23.8 %fusion.37 = f32[768,2880]{0,1:T(8,128)} fusion(f32[768,360]{0,1:T(8,128)S(1)} %fusion.19, f32[360,2880]{1,0:T(8,128)S(1)} %bitcast.101), kind=kOutput, calls=%fused_computation.94 | convolution fusion | flops 9555148800 | bytes 14100480 | tf_op jit(solution)/shard_map/dot_general | solution.py:123
  656.2 25.5 %fusion.38 = f32[768,2880]{0,1:T(8,128)} fusion(f32[768,360]{0,1:T(8,128)S(1)} %fusion.18, f32[360,2880]{1,0:T(8,128)S(1)} %bitcast.107), kind=kOutput, calls=%fused_computation.95 | convolution fusion | flops 9555148800 | bytes 14100480 | tf_op jit(solution)/shard_map/dot_general | solution.py:123
  681.7 25.1 %fusion.39 = f32[768,2880]{0,1:T(8,128)} fusion(f32[768,360]{0,1:T(8,128)S(1)} %fusion.17, f32[360,2880]{1,0:T(8,128)S(1)} %bitcast.105), kind=kOutput, calls=%fused_computation.96 | convolution fusion | flops 9555148800 | bytes 14100480 | tf_op jit(solution)/shard_map/dot_general | solution.py:123
  706.8 37.0 %add_add_fusion = f32[768,2880]{0,1:T(8,128)} fusion(f32[768,2880]{0,1:T(8,128)} %fusion.39, f32[768,2880]{0,1:T(8,128)} %fusion.38, f32[768,2880]{0,1:T(8,128)} %fusion.37, f32[768,2880]{0,1:T(8,128)} %fusion.36, f32[768,2880]{0,1:T(8,128)} %fusion.35, f32[768,2880]{0,1:T(8,128)} %fusion.33, f32[768,2880]{0,1:T(8,128)} %fusion.34, ...), kind=kOutput, calls=%fused_computation.3 | convolution fusion | flops 9570631680 | bytes 76032000 | tf_op jit(solution)/shard_map/dot_general | solution.py:123
  753.2 13.0 %copy.99 = f32[3,256,2880]{1,0,2:T(4,128)} copy(f32[3,256,2880]{2,1,0:T(8,128)} %bitcast.97) | data formatting | bytes 17694720 | tf_op jit(solution)/shard_map/reshape | solution.py:168
  771.7 130.6 %all-to-all-done.1 = f32[3,256,2880]{1,0,2:T(4,128)} async-done(((f32[3,256,2880]{1,0,2:T(4,128)}), f32[3,256,2880]{1,0,2:T(4,128)}, u32[]{:S(2)}, u32[]{:S(2)}) %all-to-all-start.1) | async-done | bytes 8847392 | tf_op jit(solution)/shard_map/all_to_all | solution.py:167
  (127 shorter events, 196.4 us)
Async XLA Ops:
  8.0 4.8 collective-permute-start
  8.4 4.4 collective-permute-start.1
  42.4 21.8 %collective-permute-start.2 = (f32[3,16,3,362]{3,1,2,0:T(8,128)S(1)}, f32[3,16,3,362]{3,1,2,0:T(8,128)}, u32[]{:S(2)}, u32[]{:S(2)}) collective-permute-start(f32[3,16,3,362]{3,1,2,0:T(8,128)S(1)} %pad_maximum_fusion.2), channel_id=1, source_target_pairs={{16,0},{20,4},{24,8},{28,12},{0,16},{4,20},{8,24},{12,28},{17,1},{... | collective-permute-start | bytes 625544 | tf_op jit(solution)/shard_map/ppermute | solution.py:32
  44.8 13.2 %collective-permute-start.4 = (f32[3,16,1,362]{3,1,2,0:T(8,128)S(1)}, f32[3,16,1,362]{3,1,2,0:T(8,128)S(1)}, u32[]{:S(2)}, u32[]{:S(2)}) collective-permute-start(f32[3,16,1,362]{3,1,2,0:T(8,128)S(1)} %copy.89), channel_id=1, source_target_pairs={{1,0},{2,1},{3,2},{5,4},{6,5},{7,6},{9,8},{10,9},{11,10},{13,12},{... | collective-permute-start | bytes 208520 | tf_op jit(solution)/shard_map/ppermute | solution.py:24
  52.5 19.8 %collective-permute-start.3 = (f32[3,16,1,362]{3,1,2,0:T(8,128)S(1)}, f32[3,16,1,362]{3,1,2,0:T(8,128)}, u32[]{:S(2)}, u32[]{:S(2)}) collective-permute-start(f32[3,16,1,362]{3,1,2,0:T(8,128)S(1)} %copy.91), channel_id=1, source_target_pairs={{0,1},{1,2},{2,3},{4,5},{5,6},{6,7},{8,9},{9,10},{10,11},{12,13},{... | collective-permute-start | bytes 208520 | tf_op jit(solution)/shard_map/ppermute | solution.py:23
  219.1 144.6 %all-to-all-start = ((f32[3,2048,360]{2,0,1:T(4,128)}), f32[3,2048,360]{2,0,1:T(4,128)}, u32[]{:S(2)}, u32[]{:S(2)}) async-start(f32[3,2048,360]{2,0,1:T(4,128)} %copy.96), calls=%async_computation | async-start | bytes 25165824 | tf_op jit(solution)/shard_map/all_to_all | solution.py:158
  388.7 41.3 %slice-start.4 = ((s8[4239360]{0:T(1024)(128)(4,1)}), s8[4194304]{0:T(1024)(128)(4,1)S(1)}, s32[]{:S(2)}) async-start(s8[4239360]{0:T(1024)(128)(4,1)} %bitcast.104), calls=%async_computation.6 | async-start | bytes 8388608
  403.0 27.0 %slice-start.5 = ((s8[4239360]{0:T(1024)(128)(4,1)}), s8[45056]{0:T(1024)(128)(4,1)S(1)}, s32[]{:S(2)}) async-start(s8[4239360]{0:T(1024)(128)(4,1)} %bitcast.104), calls=%async_computation.7 | async-start | bytes 90112
  403.0 27.0 %copy-start.13 = (f32[360]{0:T(512)S(1)}, f32[360]{0:T(512)}, u32[]{:S(2)}) copy-start(f32[360]{0:T(512)} %constant.99.clone) | copy-start | bytes 4324
  403.0 46.7 %slice-start.10 = ((s8[4239360]{0:T(1024)(128)(4,1)}), s8[4194304]{0:T(1024)(128)(4,1)S(1)}, s32[]{:S(2)}) async-start(s8[4239360]{0:T(1024)(128)(4,1)} %bitcast.110), calls=%async_computation.12 | async-start | bytes 8388608
  430.1 40.1 %slice-start.6 = ((s8[4239360]{0:T(1024)(128)(4,1)}), s8[4194304]{0:T(1024)(128)(4,1)S(1)}, s32[]{:S(2)}) async-start(s8[4239360]{0:T(1024)(128)(4,1)} %bitcast.106), calls=%async_computation.8 | async-start | bytes 8388608
  449.8 20.4 %slice-start.7 = ((s8[4239360]{0:T(1024)(128)(4,1)}), s8[45056]{0:T(1024)(128)(4,1)S(1)}, s32[]{:S(2)}) async-start(s8[4239360]{0:T(1024)(128)(4,1)} %bitcast.106), calls=%async_computation.9 | async-start | bytes 90112
  449.8 20.4 %copy-start.14 = (f32[360]{0:T(512)S(1)}, f32[360]{0:T(512)}, u32[]{:S(2)}) copy-start(f32[360]{0:T(512)} %constant.96.clone) | copy-start | bytes 4324
  449.8 40.0 %slice-start.12 = ((s8[4239360]{0:T(1024)(128)(4,1)}), s8[4194304]{0:T(1024)(128)(4,1)S(1)}, s32[]{:S(2)}) async-start(s8[4239360]{0:T(1024)(128)(4,1)} %bitcast.112), calls=%async_computation.14 | async-start | bytes 8388608
  470.2 39.8 %slice-start.2 = ((s8[4239360]{0:T(1024)(128)(4,1)}), s8[4194304]{0:T(1024)(128)(4,1)S(1)}, s32[]{:S(2)}) async-start(s8[4239360]{0:T(1024)(128)(4,1)} %bitcast.102), calls=%async_computation.4 | async-start | bytes 8388608
  521.9 23.8 %copy-start.8 = (f32[768,360]{0,1:T(8,128)S(1)}, f32[768,360]{0,1:T(8,128)}, u32[]{:S(2)}) copy-start(f32[768,360]{0,1:T(8,128)} %fusion.22) | copy-start | bytes 3317764
  545.7 25.6 %copy-start.7 = (f32[768,360]{0,1:T(8,128)S(1)}, f32[768,360]{0,1:T(8,128)}, u32[]{:S(2)}) copy-start(f32[768,360]{0,1:T(8,128)} %fusion.21) | copy-start | bytes 3317764
  545.7 49.4 %slice-start.8 = ((s8[4239360]{0:T(1024)(128)(4,1)}), s8[4194304]{0:T(1024)(128)(4,1)S(1)}, s32[]{:S(2)}) async-start(s8[4239360]{0:T(1024)(128)(4,1)} %bitcast.108), calls=%async_computation.10 | async-start | bytes 8388608
  571.3 23.7 %slice-start.9 = ((s8[4239360]{0:T(1024)(128)(4,1)}), s8[45056]{0:T(1024)(128)(4,1)S(1)}, s32[]{:S(2)}) async-start(s8[4239360]{0:T(1024)(128)(4,1)} %bitcast.108), calls=%async_computation.11 | async-start | bytes 90112
  571.3 23.7 %copy-start.6 = (f32[768,360]{0,1:T(8,128)S(1)}, f32[768,360]{0,1:T(8,128)}, u32[]{:S(2)}) copy-start(f32[768,360]{0,1:T(8,128)} %fusion.20) | copy-start | bytes 3317764
  571.3 49.2 %slice-start = ((s8[4239360]{0:T(1024)(128)(4,1)}), s8[4194304]{0:T(1024)(128)(4,1)S(1)}, s32[]{:S(2)}) async-start(s8[4239360]{0:T(1024)(128)(4,1)} %bitcast.100), calls=%async_computation.2 | async-start | bytes 8388608
  595.1 25.5 %slice-start.1 = ((s8[4239360]{0:T(1024)(128)(4,1)}), s8[45056]{0:T(1024)(128)(4,1)S(1)}, s32[]{:S(2)}) async-start(s8[4239360]{0:T(1024)(128)(4,1)} %bitcast.100), calls=%async_computation.3 | async-start | bytes 90112
  595.1 25.4 %copy-start.15 = (f32[360]{0:T(512)S(1)}, f32[360]{0:T(512)}, u32[]{:S(2)}) copy-start(f32[360]{0:T(512)} %constant.103.clone) | copy-start | bytes 4324
  766.2 136.1 %all-to-all-start.1 = ((f32[3,256,2880]{1,0,2:T(4,128)}), f32[3,256,2880]{1,0,2:T(4,128)}, u32[]{:S(2)}, u32[]{:S(2)}) async-start(f32[3,256,2880]{1,0,2:T(4,128)} %copy.99), calls=%async_computation.1 | async-start | bytes 23592960 | tf_op jit(solution)/shard_map/all_to_all | solution.py:167
  (15 other events, 156.8 us)
where the time goes:
time: 946 us; the launch traced here: 937 us
  matrix products  355 us (38%)
  waiting for transfers between devices  271 us (29%)
  local copies, waits for them, and re-layouts  176 us (19%)
  other arithmetic  110 us (12%)
  starting transfers between devices  23.5 us (2%)
    dot_general x8, matrix products, polar_filter(): jnp.dot(spectra * damping * weight[None, :], basis_rows, precision=lax.Pr...  210 us
    dot_general x8, matrix products, polar_filter(): spectra = jnp.dot(circles, basis_rows.T, precision=lax.Precision.HIGHEST)  145 us
    all_to_all x1, waiting for transfers between devices, shards(): lax.all_to_all(buffer, 'lon', split_axis=1, concat_axis=2, tiled=True)  139 us
    all_to_all x1, waiting for transfers between devices, shards(): lax.all_to_all(smoothed.reshape(item_count, row_span, lon_span), 'lon', s...  131 us
    unnamed x74, local copies, waits for them, and re-layouts  28.2 us
    add x1, other arithmetic, stencil(): view(v_wind, 0, 0) - grav_merid * (view(height, 1, 0) - view(height, 0, 0))  27.9 us
    another operation x5, local copies, waits for them, and re-layouts, stencil(): return jnp.stack([height_next, u_next, v_next])  25.8 us
    add x1, other arithmetic, stencil(): view(u_wind, 0, 0)  22.6 us
  transfers between devices with their start and end apart: 7, of which 3 were waited for; matrix products, arithmetic and copies ran while one was open for 2% of the time, Pallas kernels for 0%

commit v1 on v0

v1 whole, which is shorter than its diff:
```python
import functools
import math

import jax
import jax.numpy as jnp
import numpy as np
from jax import lax
from jax.experimental import pallas as pl
from jax.experimental.pallas import tpu as pltpu
from jax.sharding import PartitionSpec as P

grav_zonal = 0.3
grav_merid = 0.6
coriolis = 0.8
divergence_coef = 0.3
diffusion = 0.08

F32 = jnp.float32
BF16 = jnp.bfloat16
RADIX = 8


def extended(block, rim):
    return jnp.concatenate([block, rim], axis=0)


def pack_kernel(levels, h_ref, u_ref, v_ref, rim_ref, edges_ref):
    level = pl.program_id(0)

    @pl.when(level == 0)
    def _():
        edges_ref[...] = jnp.zeros_like(edges_ref)

    lane = lax.broadcasted_iota(jnp.int32, edges_ref.shape, 1)
    last = edges_ref.shape[1] - 1
    edges = edges_ref[...]
    for field, ref in enumerate((h_ref, u_ref, v_ref)):
        whole = extended(ref[0], rim_ref[field, 0])
        low = whole[:, 0:1]
        high = whole[:, last : last + 1]
        edges = jnp.where(lane == field * levels + level, low, edges)
        edges = jnp.where(lane == (3 + field) * levels + level, high, edges)
        if field == 2:
            edges = jnp.where(lane == 6 * levels + level, whole[:, last - 1 : last], edges)
    edges_ref[...] = edges


def stencil_kernel(levels, h_ref, u_ref, v_ref, rim_ref, south_ref, north_ref, coef_ref, out_ref):
    level = pl.program_id(0)
    rows = h_ref.shape[1]
    shape = south_ref.shape
    lane = lax.broadcasted_iota(jnp.int32, shape, 1)
    width = shape[1]
    south_edges = south_ref[...]
    north_edges = north_ref[...]

    def east(x):
        return pltpu.roll(x, shape[0] - 1, 0)

    def west(x):
        return pltpu.roll(x, 1, 0)

    def south(x, field):
        edge = pltpu.roll(south_edges, lax.rem(width - (field * levels + level), width), 1)
        return jnp.where(lane == 0, edge, pltpu.roll(x, 1, 1))

    def north(x, field):
        edge = pltpu.roll(north_edges, width - 1 - (field * levels + level), 1)
        return jnp.where(lane == width - 1, edge, pltpu.roll(x, width - 1, 1))

    h = extended(h_ref[0], rim_ref[0, 0])
    u = extended(u_ref[0], rim_ref[1, 0])
    v = extended(v_ref[0], rim_ref[2, 0])
    inverse_cos = coef_ref[0:1]
    sin_center = coef_ref[1:2]
    sin_face = coef_ref[2:3]
    cos_face = coef_ref[3:4]
    cos_south = coef_ref[4:5]
    h_south, h_north = south(h, 0), north(h, 0)
    u_south, u_north = south(u, 1), north(u, 1)
    v_south, v_north = south(v, 2), north(v, 2)
    h_east, u_west = east(h), west(u)
    v_pair = v + v_south
    u_pair = u + u_north
    u_lap = east(u) + u_west + u_north + u_south - 4.0 * u
    v_lap = east(v) + west(v) + v_north + v_south - 4.0 * v
    h_lap = h_east + west(h) + h_north + h_south - 4.0 * h
    u_step = (
        u
        - (grav_zonal * inverse_cos) * (h_east - h)
        + (coriolis * 0.25 * sin_center) * (v_pair + east(v_pair))
        + diffusion * u_lap
    )
    v_step = (
        v
        - grav_merid * (h_north - h)
        - (coriolis * 0.25 * sin_face) * (u_pair + west(u_pair))
        + diffusion * v_lap
    )
    flux = u - u_west + cos_face * v - cos_south * v_south
    h_step = h - (divergence_coef * inverse_cos) * flux + diffusion * h_lap
    out_ref[0, 0] = h_step[:rows]
    out_ref[1, 0] = u_step[:rows]
    out_ref[2, 0] = v_step[:rows]


def split(x):
    high = x.astype(BF16)
    return high, (x - high.astype(F32)).astype(BF16)


def triple_dot(high, low, x):
    x_high, x_low = split(x)
    return (
        jnp.dot(high, x_high, preferred_element_type=F32)
        + jnp.dot(high, x_low, preferred_element_type=F32)
        + jnp.dot(low, x_high, preferred_element_type=F32)
    )


def forward_parts(x):
    half = math.sqrt(0.5)
    a = [x[p] + x[p + 4] for p in range(4)]
    b = [x[p] - x[p + 4] for p in range(4)]
    even, odd = a[0] + a[2], a[1] + a[3]
    minus, plus = half * (b[1] - b[3]), half * (b[1] + b[3])
    return [
        (even + odd,),
        (b[0] + minus, -(b[2] + plus)),
        (a[0] - a[2], a[3] - a[1]),
        (b[0] - minus, b[2] - plus),
        (even - odd,),
    ]


def inverse_parts(z):
    half = math.sqrt(0.5)
    z0, z4 = z[0][0], z[4][0]
    (r1, i1), (r2, i2), (r3, i3) = z[1], z[2], z[3]
    even_p, even_m = z0 + z4 + r2, z0 + z4 - r2
    odd_p, odd_m = z0 - z4 - i2, z0 - z4 + i2
    c0 = r1 + r3
    c1 = half * (r1 - i1 - r3 - i3)
    c2 = i3 - i1
    c3 = half * (r3 - i3 - r1 - i1)
    base = [even_p, odd_p, even_m, odd_m]
    waves = [c0, c1, c2, c3]
    return [base[p] + waves[p] for p in range(4)] + [base[p] - waves[p] for p in range(4)]


def filter_kernel(x_ref, fh_ref, fl_ref, gh_ref, gl_ref, eh_ref, el_ref, ih_ref, il_ref, damp_ref, out_ref):
    n_lon, pair, cols, width = x_ref.shape
    group = n_lon // RADIX
    span = group * cols
    blocks = [
        jnp.concatenate(
            [
                jnp.concatenate([x_ref[p * group + j, item] for item in range(pair)], axis=1)
                for j in range(group)
            ],
            axis=0,
        )
        for p in range(RADIX)
    ]
    parts = forward_parts(blocks)
    waves = []
    first = 0
    for kind in range(5):
        if kind in (0, 4):
            slot = kind // 4
            y = parts[kind][0]
            count = span
            fh, fl, gh, gl = eh_ref[slot], el_ref[slot], ih_ref[slot], il_ref[slot]
        else:
            slot = kind - 1
            y = jnp.concatenate(parts[kind], axis=0)
            count = 2 * span
            fh, fl, gh, gl = fh_ref[slot], fl_ref[slot], gh_ref[slot], gl_ref[slot]
        damp = damp_ref[first : first + count]
        first += count
        spectrum = triple_dot(fh, fl, y) * jnp.concatenate([damp] * pair, axis=1)
        z = triple_dot(gh, gl, spectrum)
        waves.append((z,) if count == span else (z[:span], z[span:]))
    for p, block in enumerate(inverse_parts(waves)):
        for j in range(group):
            for item in range(pair):
                out_ref[p * group + j, item] = block[
                    j * cols : (j + 1) * cols, item * width : (item + 1) * width
                ]


def fourier_tables(lon_total):
    span = lon_total // RADIX
    q = np.arange(span)
    real_tables, complex_tables = [], []
    wavenums, weights = [], []
    for kind in range(5):
        if kind == 0:
            k_cos = RADIX * np.arange(span // 2 + 1)
            k_sin = RADIX * np.arange(1, span // 2)
        elif kind == 4:
            k_cos = k_sin = RADIX * np.arange(span // 2) + 4
        else:
            k_cos = k_sin = RADIX * np.arange(span) + kind
        cos_rows = np.cos((k_cos[:, None] * q % lon_total) * (2.0 * math.pi / lon_total))
        sin_rows = np.sin((k_sin[:, None] * q % lon_total) * (2.0 * math.pi / lon_total))
        if kind in (0, 4):
            real_tables.append(np.concatenate([cos_rows, sin_rows], 0))
        else:
            complex_tables.append(np.block([[cos_rows, sin_rows], [-sin_rows, cos_rows]]))
        k_all = np.concatenate([k_cos, k_sin])
        wavenums.append(k_all)
        weights.append(np.where((k_all == 0) | (k_all == lon_total // 2), 1.0, 2.0) / lon_total)
    wavenums = np.concatenate(wavenums)
    sine_sq = np.sin(wavenums * (math.pi / lon_total)) ** 2

    def halves(tables):
        table = np.stack(tables).astype(np.float32)
        high = table.astype(jnp.bfloat16)
        low = (table - high.astype(np.float32)).astype(jnp.bfloat16)
        turn = lambda t: np.ascontiguousarray(np.swapaxes(t, 1, 2))
        return high, low, turn(high), turn(low)

    return halves(complex_tables), halves(real_tables), sine_sq, np.concatenate(weights)


def latitude_table(rows, lat_total):
    g = np.arange(lat_total)
    cos_center = np.sin((g + 0.5) * math.pi / lat_total)
    table = np.zeros((8, lat_total))
    table[0] = 1.0 / cos_center
    table[1] = -np.cos((g + 0.5) * math.pi / lat_total)
    table[2] = -np.cos((g + 1.0) * math.pi / lat_total)
    table[3] = np.where(g + 1 < lat_total, np.sin((g + 1.0) * math.pi / lat_total), 0.0)
    table[4] = np.sin(g * math.pi / lat_total)
    table[5] = 2.0 * cos_center * cos_center
    return table.reshape(8, lat_total // rows, rows).swapaxes(0, 1).astype(np.float32)


def ring(axis, step, wrap=True):
    size = lax.axis_size(axis)
    return [(i, (i + step) % size) for i in range(size) if wrap or 0 <= i + step < size]


def shards(u_wind, v_wind, height):
    levels, cols, rows = height.shape
    n_lat, n_lon = lax.axis_size("lat"), lax.axis_size("lon")
    lat_total, lon_total = rows * n_lat, cols * n_lon
    band = lax.axis_index("lat")
    fields = (height, u_wind, v_wind)
    ext = -(-(cols + 2) // 8) * 8
    spare = ext - cols

    lasts = jnp.stack([f[:, cols - 1] for f in fields])
    firsts = jnp.stack([f[:, 0] for f in fields])
    west_rim = lax.ppermute(lasts, "lon", ring("lon", 1))
    east_rim = lax.ppermute(firsts, "lon", ring("lon", -1))
    middle = jnp.zeros((3, levels, spare - 2, rows), F32)
    rim = jnp.concatenate([east_rim[:, :, None], middle, west_rim[:, :, None]], 2)

    level_spec = pl.BlockSpec((1, cols, rows), lambda l: (l, 0, 0))
    rim_spec = pl.BlockSpec((3, 1, spare, rows), lambda l: (0, l, 0, 0))
    edge_spec = pl.BlockSpec((ext, rows), lambda l: (0, 0))
    edges = pl.pallas_call(
        functools.partial(pack_kernel, levels),
        grid=(levels,),
        in_specs=[level_spec] * 3 + [rim_spec],
        out_specs=edge_spec,
        out_shape=jax.ShapeDtypeStruct((ext, rows), F32),
        compiler_params=pltpu.CompilerParams(vmem_limit_bytes=32 * 1024 * 1024),
    )(*fields, rim)

    from_south = lax.ppermute(edges, "lat", ring("lat", 1, False))
    from_north = lax.ppermute(edges, "lat", ring("lat", -1, False))
    across = lax.ppermute(edges, "lon", ring("lon", n_lon // 2))
    count = levels
    pad = jnp.zeros((ext, rows - 3 * count), F32)
    south_wall = jnp.concatenate(
        [across[:, :count], -across[:, count : 2 * count], jnp.zeros((ext, count), F32)], 1
    )
    north_wall = jnp.concatenate(
        [
            across[:, 3 * count : 4 * count],
            -across[:, 4 * count : 5 * count],
            -across[:, 6 * count : 7 * count],
        ],
        1,
    )
    south_edges = jnp.where(band == 0, south_wall, from_south[:, 3 * count : 6 * count])
    north_edges = jnp.where(band == n_lat - 1, north_wall, from_north[:, : 3 * count])
    south_edges = jnp.concatenate([south_edges, pad], 1)
    north_edges = jnp.concatenate([north_edges, pad], 1)

    coef = lax.dynamic_index_in_dim(jnp.asarray(latitude_table(rows, lat_total)), band, 0, False)
    stepped = pl.pallas_call(
        functools.partial(stencil_kernel, levels),
        grid=(levels,),
        in_specs=[level_spec] * 3
        + [rim_spec, edge_spec, edge_spec, pl.BlockSpec((8, rows), lambda l: (0, 0))],
        out_specs=pl.BlockSpec((3, 1, cols, rows), lambda l: (0, l, 0, 0)),
        out_shape=jax.ShapeDtypeStruct((3, levels, cols, rows), F32),
        compiler_params=pltpu.CompilerParams(vmem_limit_bytes=40 * 1024 * 1024),
    )(*fields, rim, south_edges, north_edges, coef)

    items = 3 * levels // n_lon
    pair = 2 if items % 2 == 0 else 1
    arrived = lax.all_to_all(
        stepped.reshape(n_lon, items, cols, rows), "lon", split_axis=0, concat_axis=0
    )
    complex_tables, real_tables, sine_sq, weight = fourier_tables(lon_total)
    ratio = coef[5][None, :]
    damp = (
        jnp.asarray(weight, F32)[:, None]
        * ratio
        / jnp.maximum(jnp.asarray(sine_sq, F32)[:, None], ratio)
    )
    item_spec = pl.BlockSpec((n_lon, pair, cols, rows), lambda i: (0, i, 0, 0))
    whole = pl.BlockSpec(memory_space=pltpu.VMEM)
    smoothed = pl.pallas_call(
        filter_kernel,
        grid=(items // pair,),
        in_specs=[item_spec] + [whole] * 9,
        out_specs=item_spec,
        out_shape=jax.ShapeDtypeStruct((n_lon, items, cols, rows), F32),
        compiler_params=pltpu.CompilerParams(vmem_limit_bytes=56 * 1024 * 1024),
    )(
        arrived,
        *(jnp.asarray(t) for t in complex_tables),
        *(jnp.asarray(t) for t in real_tables),
        damp,
    )
    returned = lax.all_to_all(smoothed, "lon", split_axis=0, concat_axis=0)
    returned = returned.reshape(3, levels, cols, rows)
    is_polar = (band < n_lat // 4) | (band >= n_lat - n_lat // 4)
    result = [jnp.where(is_polar, returned[f], stepped[f]) for f in range(3)]
    return result[1], result[2], result[0]


def solution(mesh):
    placed = (P(None, "lon", "lat"),) * 3
    return jax.shard_map(shards, mesh=mesh, in_specs=placed, out_specs=placed, check_vma=False)
```

time: 946 us -> 305 us (0.32)
  matrix products: 355 us -> 0 us
  local copies, waits for them, and re-layouts: 176 us -> 12.7 us
  other arithmetic: 110 us -> 13.2 us
  waiting for transfers between devices: 271 us -> 201 us
  Pallas kernels: 0 us -> 54.8 us
    dot_general x16 -> x0, matrix products: 355 us -> none  [the longest x8 210 us: polar_filter(): jnp.dot(spectra * damping * weight[None, :], basis_rows, precision=lax.Pr...]
    all_to_all x2, waiting for transfers between devices: 270 us -> 195 us  [the longest x1 99 us: shards(): returned = lax.all_to_all(smoothed, 'lon', split_axis=0, concat_axis=0)]
    add x3 -> x0, other arithmetic: 66.2 us -> none  [the longest x1 27.9 us: stencil(): view(v_wind, 0, 0) - grav_merid * (view(height, 1, 0) - view(height, 0, 0))]
    pallas_call x0 -> x3, Pallas kernels: none -> 54.8 us  [the longest x1 33.8 us: shards(): pl.pallas_call(filter_kernel, grid=(items // pair,), in_specs=[item_spec]...]
    slice x5 -> x3, local copies, waits for them, and re-layouts: 32.8 us -> 2.66 us  [shards(): firsts = jnp.stack([f[:, 0] for f in fields])]
    another operation x8 -> x0, local copies, waits for them, and re-layouts: 27 us -> none  [the longest x5 25.8 us: stencil(): return jnp.stack([height_next, u_next, v_next])]
    all_to_all x3 -> x0, local copies, waits for them, and re-layouts: 24.5 us -> none  [the longest x1 13.6 us: shards(): lax.all_to_all(buffer, 'lon', split_axis=1, concat_axis=2, tiled=True)]
    reshape x2 -> x0, local copies, waits for them, and re-layouts: 24.5 us -> none  [the longest x1 13 us: shards(): smoothed.reshape(item_count, row_span, lon_span)]
  transfers between devices with their start and end apart: 7 -> 7, of which waited for: 3 -> 5; matrix products, arithmetic and copies ran while one was open for 2% -> 1% of each run, Pallas kernels for 0% -> 0%
where the time goes in v1:
time: 305 us; the launch traced here: 304 us
  waiting for transfers between devices  201 us (66%)
  Pallas kernels  54.8 us (18%)
  starting transfers between devices  21.6 us (7%)
  other arithmetic  13.2 us (4%)
  local copies, waits for them, and re-layouts  12.7 us (4%)
    all_to_all x1, waiting for transfers between devices, shards(): returned = lax.all_to_all(smoothed, 'lon', split_axis=0, concat_axis=0)  99 us
    all_to_all x1, waiting for transfers between devices, shards(): lax.all_to_all(stepped.reshape(n_lon, items, cols, rows), 'lon', split_ax...  96.4 us
    pallas_call x1, Pallas kernels, shards(): pl.pallas_call(filter_kernel, grid=(items // pair,), in_specs=[item_spec]...  33.8 us
    pallas_call x1, Pallas kernels, shards(): pl.pallas_call(functools.partial(stencil_kernel, levels), grid=(levels,),...  14.1 us
    select_n x1, other arithmetic, shards(): result = [jnp.where(is_polar, returned[f], stepped[f]) for f in range(3)]  9.96 us
    unnamed x16, local copies, waits for them, and re-layouts  9.17 us
    pallas_call x1, Pallas kernels, shards(): pl.pallas_call(functools.partial(pack_kernel, levels), grid=(levels,), in...  6.91 us
  transfers between devices with their start and end apart: 7, of which 5 were waited for; matrix products, arithmetic and copies ran while one was open for 1% of the time, Pallas kernels for 0%

profile of v1, /device:TPU:0, one launch (start us, length us, event | category | flops | bytes accessed | tf_op | source)
XLA Modules:
  0.0 304.0 jit_solution(14611902241019498956)
XLA Ops:
  0.6 0.9 fusion.4
  1.5 0.9 fusion.5
  2.4 0.9 fusion.3
  3.8 3.0 collective-permute-start
  6.9 1.4 collective-permute-done.1
  8.4 1.8 copy-done
  10.2 1.8 copy-done.2
  12.1 1.8 copy-done.4
  13.9 6.9 %shard_map.157 = f32[368,128]{1,0:T(8,128)S(1)} custom-call(f32[16,360,128]{2,1,0:T(8,128)S(1)} %copy-done, f32[16,360,128]{2,1,0:T(8,128)S(1)} %copy-done.2, f32[16,360,128]{2,1,0:T(8,128)S(1)} %copy-done.4, f32[3,16,8,128]{3,2,1,0:T(8,128)S(1)} %pad_maximum_fusion.rim_ref), custom_call_target="tpu_custom_call" | custom-call | tf_op jit(solution)/shard_map/pallas_call | solution.py:264
  20.8 2.3 collective-permute-start.2
  23.2 0.7 constant_dynamic-slice_fusion
  23.9 1.3 collective-permute-start.4
  25.1 4.6 %collective-permute-start.3 = (f32[368,128]{1,0:T(8,128)S(1)}, f32[368,128]{1,0:T(8,128)S(1)}, u32[]{:S(2)}, u32[]{:S(2)}) collective-permute-start(f32[368,128]{1,0:T(8,128)S(1)} %shard_map.157), channel_id=1, source_target_pairs={{0,1},{1,2},{2,3},{4,5},{5,6},{6,7},{8,9},{9,10},{10,11},{12,13},{... | collective-permute-start | bytes 565256 | tf_op jit(solution)/shard_map/ppermute | solution.py:273
  30.0 4.0 %collective-permute-done.3 = f32[368,128]{1,0:T(8,128)S(1)} collective-permute-done((f32[368,128]{1,0:T(8,128)S(1)}, f32[368,128]{1,0:T(8,128)S(1)}, u32[]{:S(2)}, u32[]{:S(2)}) %collective-permute-start.3) | collective-permute-done | bytes 188448 | tf_op jit(solution)/shard_map/ppermute | solution.py:273
  34.4 1.8 copy-done.3
  36.2 1.8 copy-done.5
  38.1 14.1 %shard_map.158 = f32[3,16,360,128]{3,2,1,0:T(8,128)} custom-call(f32[16,360,128]{2,1,0:T(8,128)S(1)} %copy-done.1, f32[16,360,128]{2,1,0:T(8,128)S(1)} %copy-done.3, f32[16,360,128]{2,1,0:T(8,128)S(1)} %copy-done.5, f32[3,16,8,128]{3,2,1,0:T(8,128)S(1)} %pad_maximum_fusion.rim_ref, f32[368,128]{1,0:T(8,128)S(1)} %concatenate.17.south_ref, ...), custom_call_target="tpu_custom_call" | custom-call | tf_op jit(solution)/shard_map/pallas_call | solution.py:295
  52.1 5.1 %all-to-all-start = ((f32[8,6,360,128]{3,2,1,0:T(8,128)}), f32[8,6,360,128]{3,2,1,0:T(8,128)}, u32[]{:S(2)}, u32[]{:S(2)}) async-start(f32[8,6,360,128]{3,2,1,0:T(8,128)} %bitcast.32), calls=%async_computation | async-start | bytes 17694720 | tf_op jit(solution)/shard_map/all_to_all | solution.py:307
  57.3 2.5 maximum_divide_fusion.damp_ref
  59.8 96.4 %all-to-all-done.x_ref = f32[8,6,360,128]{3,2,1,0:T(8,128)} async-done(((f32[8,6,360,128]{3,2,1,0:T(8,128)}), f32[8,6,360,128]{3,2,1,0:T(8,128)}, u32[]{:S(2)}, u32[]{:S(2)}) %all-to-all-start) | async-done | bytes 8847392 | tf_op jit(solution)/shard_map/all_to_all | solution.py:307
  156.2 33.8 %shard_map.159 = f32[8,6,360,128]{3,2,1,0:T(8,128)} custom-call(f32[8,6,360,128]{3,2,1,0:T(8,128)} %all-to-all-done.x_ref, bf16[3,720,720]{2,1,0:T(8,128)(2,1)} %constant.44.clone.fh_ref, bf16[3,720,720]{2,1,0:T(8,128)(2,1)} %constant.45.clone.fl_ref, bf16[3,720,720]{2,1,0:T(8,128)(2,1)} %constant.46.clone.gh_ref, ...), custom_call_target="tpu_custom_call" | custom-call | tf_op jit(solution)/shard_map/pallas_call | solution.py:319
  190.0 5.0 %all-to-all-start.1 = ((f32[8,6,360,128]{3,2,1,0:T(8,128)}), f32[8,6,360,128]{3,2,1,0:T(8,128)}, u32[]{:S(2)}, u32[]{:S(2)}) async-start(f32[8,6,360,128]{3,2,1,0:T(8,128)} %shard_map.159), calls=%async_computation.1 | async-start | bytes 17694720 | tf_op jit(solution)/shard_map/all_to_all | solution.py:332
  195.0 99.0 %all-to-all-done.1 = f32[8,6,360,128]{3,2,1,0:T(8,128)} async-done(((f32[8,6,360,128]{3,2,1,0:T(8,128)}), f32[8,6,360,128]{3,2,1,0:T(8,128)}, u32[]{:S(2)}, u32[]{:S(2)}) %all-to-all-start.1) | async-done | bytes 8847392 | tf_op jit(solution)/shard_map/all_to_all | solution.py:332
  294.0 10.0 %fusion = (f32[16,360,128]{2,1,0:T(8,128)}, f32[16,360,128]{2,1,0:T(8,128)}, f32[16,360,128]{2,1,0:T(8,128)}) fusion(f32[3,16,360,128]{3,2,1,0:T(8,128)} %shard_map.158, f32[3,16,360,128]{3,2,1,0:T(8,128)} %bitcast.11, pred[]{:T(512)S(6)} %or.3), kind=kLoop, calls=%fused_computation.1 | loop fusion | flops 2211840 | bytes 26542080 | tf_op jit(solution)/shard_map/jit(_where)/select_n | solution.py:335
  (28 shorter events, 1.5 us)
Async XLA Ops:
  3.3 4.9 %collective-permute-start.1 = (f32[3,16,128]{2,1,0:T(8,128)S(1)}, f32[3,16,128]{2,1,0:T(8,128)S(1)}, u32[]{:S(2)}, u32[]{:S(2)}) collective-permute-start(f32[3,16,128]{2,1,0:T(8,128)S(1)} %pad_maximum_fusion.2), channel_id=1, source_target_pairs={{0,4},{4,8},{8,12},{12,16},{16,20},{20,24},{24,28},{28,0},{1,5},{5... | collective-permute-start | bytes 73736 | tf_op jit(solution)/shard_map/ppermute | solution.py:256
  3.8 4.5 %collective-permute-start = (f32[3,16,128]{2,1,0:T(8,128)S(1)}, f32[3,16,128]{2,1,0:T(8,128)S(1)}, u32[]{:S(2)}, u32[]{:S(2)}) collective-permute-start(f32[3,16,128]{2,1,0:T(8,128)S(1)} %pad_maximum_fusion.1), channel_id=1, source_target_pairs={{0,28},{4,0},{8,4},{12,8},{16,12},{20,16},{24,20},{28,24},{1,29},{... | collective-permute-start | bytes 73736 | tf_op jit(solution)/shard_map/ppermute | solution.py:257
  8.4 1.8 copy-start
  10.2 1.8 copy-start.2
  12.1 1.8 copy-start.4
  20.8 13.6 %copy-start.1 = (f32[16,360,128]{2,1,0:T(8,128)S(1)}, f32[16,360,128]{2,1,0:T(8,128)}, u32[]{:S(2)}) copy-start(f32[16,360,128]{2,1,0:T(8,128)} %h_ref.3) | copy-start | bytes 8847364
  20.8 8.9 %collective-permute-start.2 = (f32[368,128]{1,0:T(8,128)S(1)}, f32[368,128]{1,0:T(8,128)S(1)}, u32[]{:S(2)}, u32[]{:S(2)}) collective-permute-start(f32[368,128]{1,0:T(8,128)S(1)} %shard_map.157), channel_id=1, source_target_pairs={{0,16},{4,20},{8,24},{12,28},{16,0},{20,4},{24,8},{28,12},{1,17},{... | collective-permute-start | bytes 565256 | tf_op jit(solution)/shard_map/ppermute | solution.py:275
  23.9 10.3 %collective-permute-start.4 = (f32[368,128]{1,0:T(8,128)S(1)}, f32[368,128]{1,0:T(8,128)S(1)}, u32[]{:S(2)}, u32[]{:S(2)}) collective-permute-start(f32[368,128]{1,0:T(8,128)S(1)} %shard_map.157), channel_id=1, source_target_pairs={{1,0},{2,1},{3,2},{5,4},{6,5},{7,6},{9,8},{10,9},{11,10},{13,12},{... | collective-permute-start | bytes 565256 | tf_op jit(solution)/shard_map/ppermute | solution.py:274
  25.1 8.8 %collective-permute-start.3 = (f32[368,128]{1,0:T(8,128)S(1)}, f32[368,128]{1,0:T(8,128)S(1)}, u32[]{:S(2)}, u32[]{:S(2)}) collective-permute-start(f32[368,128]{1,0:T(8,128)S(1)} %shard_map.157), channel_id=1, source_target_pairs={{0,1},{1,2},{2,3},{4,5},{5,6},{6,7},{8,9},{9,10},{10,11},{12,13},{... | collective-permute-start | bytes 565256 | tf_op jit(solution)/shard_map/ppermute | solution.py:273
  34.4 1.8 copy-start.3
  36.2 1.8 copy-start.5
  52.1 5.1 %copy-start.6 = (f32[2880]{0:T(1024)S(1)}, f32[2880]{0:T(1024)}, u32[]{:S(2)}) copy-start(f32[2880]{0:T(1024)} %constant.43.clone) | copy-start | bytes 34564
  52.1 5.1 %copy-start.7 = (f32[2880]{0:T(1024)S(1)}, f32[2880]{0:T(1024)}, u32[]{:S(2)}) copy-start(f32[2880]{0:T(1024)} %constant.42.clone) | copy-start | bytes 34564
  52.1 104.1 %all-to-all-start = ((f32[8,6,360,128]{3,2,1,0:T(8,128)}), f32[8,6,360,128]{3,2,1,0:T(8,128)}, u32[]{:S(2)}, u32[]{:S(2)}) async-start(f32[8,6,360,128]{3,2,1,0:T(8,128)} %bitcast.32), calls=%async_computation | async-start | bytes 17694720 | tf_op jit(solution)/shard_map/all_to_all | solution.py:307
  190.0 104.0 %all-to-all-start.1 = ((f32[8,6,360,128]{3,2,1,0:T(8,128)}), f32[8,6,360,128]{3,2,1,0:T(8,128)}, u32[]{:S(2)}, u32[]{:S(2)}) async-start(f32[8,6,360,128]{3,2,1,0:T(8,128)} %shard_map.159), calls=%async_computation.1 | async-start | bytes 17694720 | tf_op jit(solution)/shard_map/all_to_all | solution.py:332
